TPU v7x, 32 devices: a whole 2x2x4 slice. The times are simulated.
32 devices in a mesh: groups: 2 (over x), dp: 16 (over z, y, core).
Axes of the slice: x: 2, y: 2, z: 4, core: 2. Of those that a mesh axis runs over, the one named last changes fastest.
Arguments:
- tokens: bfloat16 [256, 16384], P(('groups', 'dp')), parts along dimension 0, may hold values from -6 to 6
- gain: bfloat16 [16384], replicated, may hold values from 0.099609375 to 1.8984375
- gate_weight: bfloat16 [16384, 8192], P(None, 'dp'), may hold values from -0.046875 to 0.046875
- up_weight: bfloat16 [16384, 8192], P(None, 'dp'), may hold values from -0.046875 to 0.046875
- down_weight: bfloat16 [8192, 16384], P(None, 'dp'), may hold values from -0.125 to 0.125
Outputs:
- mixed: bfloat16 [256, 16384], P(('groups', 'dp')), parts along dimension 0
There are 2 independent parts, one for each index of `groups`. A program takes and returns all parts, laid end to end along the dimension named above; an argument that names none is the same for every part. Nothing has to cross between parts.
All inputs are finite; a program needn't handle non-finite values.
Results may differ from a plain program's by a relative error of at most 0.006.
Values may be sent and summed in bfloat16 or wider, within the bound.
A program may use at most 128 MiB of HBM per device.

v0:
```python
import jax
import jax.numpy as jnp
from jax import lax
from jax.sharding import PartitionSpec as P


def shards(tokens, gain, gate_weight, up_weight, down_weight):
    wide = tokens.astype(jnp.float32)
    scale = lax.rsqrt(jnp.mean(wide * wide, axis=-1, keepdims=True) + 1e-05)
    normed = (wide * scale * gain.astype(jnp.float32)).astype(jnp.bfloat16)
    piece = lax.all_gather(normed, "dp", axis=0, tiled=True)
    gate = jnp.dot(piece, gate_weight, preferred_element_type=jnp.float32)
    up = jnp.dot(piece, up_weight, preferred_element_type=jnp.float32)
    hidden = (jax.nn.silu(gate) * up).astype(jnp.bfloat16)
    columns = jnp.dot(
        lax.all_gather(hidden, "dp", axis=1, tiled=True),
        down_weight,
        preferred_element_type=jnp.float32,
    )
    total = lax.all_to_all(columns, "dp", split_axis=0, concat_axis=1, tiled=True)
    return (wide + total).astype(jnp.bfloat16)


def solution(mesh):
    return jax.shard_map(
        shards,
        mesh=mesh,
        in_specs=(P(("groups", "dp"), None), P(), P(None, "dp"), P(None, "dp"), P(None, "dp")),
        out_specs=P(("groups", "dp"), None),
        check_vma=False,
    )
```

profile of v0, /device:TPU:0, one launch (start us, length us, event | category | flops | bytes accessed | tf_op | source)
XLA Modules:
  0.0 154.0 jit_solution(4118281689761961317)
XLA Ops:
  6.5 0.0 all-gather.3.cloned.1.call-start
  6.5 1.2 fusion.1
  7.7 0.8 convert_element_type.16
  8.5 1.8 %fusion.3 = bf16[8,16384]{1,0:T(8,128)(2,1)} fusion(bf16[8,16384]{1,0:T(8,128)(2,1)} %param.5, f32[16384]{0:T(1024)S(1)} %convert_element_type.16, f32[8]{0:T(128)S(1)} %add_rsqrt_fusion), kind=kLoop, calls=%fused_computation.8 | loop fusion | flops 524288 | bytes 589856 | tf_op jit(solution)/shard_map/convert_element_type | solution.py:10
  10.3 0.0 all-gather.3.cloned.1.call-update
  10.3 0.0 all-gather.5.cloned.1.call-start
  10.4 53.4 %all-gather.3.cloned.1.call-done = bf16[128,16384]{1,0:T(8,128)(2,1)} async-done(((bf16[8,16384]{1,0:T(8,128)(2,1)}), bf16[128,16384]{1,0:T(8,128)(2,1)}) %all-gather.3.cloned.1.call-update) | async-done | bytes 4194320 | tf_op jit(solution)/shard_map/all_gather | solution.py:11
  63.7 0.0 copy-start
  63.7 0.0 copy-start.1
  63.7 9.5 %fusion.5 = f32[128,512]{1,0:T(8,128)S(1)} fusion(bf16[128,16384]{1,0:T(8,128)(2,1)} %all-gather.3.cloned.1.call-done, bf16[16384,512]{1,0:T(8,128)(2,1)} %param.7), kind=kOutput, calls=%fused_computation.11 | convolution fusion | flops 2147483648 | bytes 21233664 | tf_op jit(solution)/shard_map/dot_general | solution.py:12
  73.3 0.0 copy-done
  73.3 3.6 %copy-done.1 = bf16[16384,512]{1,0:T(8,128)(2,1)S(1)} copy-done((bf16[16384,512]{1,0:T(8,128)(2,1)S(1)}, bf16[16384,512]{1,0:T(8,128)(2,1)}, u32[]{:S(2)}) %copy-start.1) | copy-done | bytes 16777240
  76.8 3.0 %fusion = bf16[128,512]{1,0:T(8,128)(2,1)} fusion(bf16[128,16384]{1,0:T(8,128)(2,1)S(1)} %copy-done, bf16[16384,512]{1,0:T(8,128)(2,1)S(1)} %copy-done.1, f32[128,512]{1,0:T(8,128)S(1)} %fusion.5), kind=kOutput, calls=%fused_computation.2 | convolution fusion | flops 2147876864 | bytes 21364736 | tf_op jit(solution)/shard_map/dot_general | solution.py:13
  79.8 0.0 copy-start.2
  79.8 0.0 all-gather.5.cloned.1.call-update
  79.8 39.8 %all-gather.5.cloned.1.call-done = bf16[128,8192]{1,0:T(8,128)(2,1)} async-done(((bf16[128,512]{1,0:T(8,128)(2,1)}), bf16[128,8192]{1,0:T(8,128)(2,1)}) %all-gather.5.cloned.1.call-update) | async-done | bytes 2097168 | tf_op jit(solution)/shard_map/all_gather | solution.py:16
  119.7 8.7 %convolution_bitcast_fusion = f32[16,8,1024]{2,1,0:T(8,128)S(1)} fusion(bf16[128,8192]{1,0:T(8,128)(2,1)} %all-gather.5.cloned.1.call-done, bf16[8192,1024]{1,0:T(8,128)(2,1)} %param.9), kind=kOutput, calls=%fused_computation | convolution fusion | flops 2147483648 | bytes 19398656 | tf_op jit(solution)/shard_map/dot_general | solution.py:15
  128.4 17.9 %all_to_all.19 = f32[16,8,1024]{2,1,0:T(8,128)S(1)} all-to-all(f32[16,8,1024]{2,1,0:T(8,128)S(1)} %convolution_bitcast_fusion), channel_id=1, replica_groups=mesh['groups'=2,'dp'=16] {'dp'}, dimensions={0} | all-to-all | bytes 1048576 | tf_op jit(solution)/shard_map/all_to_all | solution.py:20
  146.3 0.0 copy-done.2
  146.3 0.8 fusion.4
  (1 shorter events, 0.0 us)
Async XLA Ops:
  6.5 57.2 %all-gather.3.cloned.1.call-start = ((), (), s32[]{:S(2)}) async-start(), calls=%async_computation.1 | async-start | bytes 4456448 | tf_op jit(solution)/shard_map/all_gather | solution.py:11
  10.3 109.4 %all-gather.5.cloned.1.call-start = ((), (), s32[]{:S(2)}) async-start(), calls=%async_computation.2 | async-start | bytes 2228224 | tf_op jit(solution)/shard_map/all_gather | solution.py:16
  63.7 9.5 %copy-start = (bf16[128,16384]{1,0:T(8,128)(2,1)S(1)}, bf16[128,16384]{1,0:T(8,128)(2,1)}, u32[]{:S(2)}) copy-start(bf16[128,16384]{1,0:T(8,128)(2,1)} %all-gather.3.cloned.1.call-done) | copy-start | bytes 12582916
  63.7 13.1 %copy-start.1 = (bf16[16384,512]{1,0:T(8,128)(2,1)S(1)}, bf16[16384,512]{1,0:T(8,128)(2,1)}, u32[]{:S(2)}) copy-start(bf16[16384,512]{1,0:T(8,128)(2,1)} %param.8) | copy-start | bytes 50331652
  79.8 66.5 %copy-start.2 = (bf16[8,16384]{1,0:T(8,128)(2,1)S(1)}, bf16[8,16384]{1,0:T(8,128)(2,1)}, u32[]{:S(2)}) copy-start(bf16[8,16384]{1,0:T(8,128)(2,1)} %param.5) | copy-start | bytes 786436
Sparse Core Ops, SparseCore 0:
  10.4 53.2 all-gather.2
  80.0 39.6 all-gather.4
where the time goes:
time: 154 us
  waiting for transfers between devices  93.2 us (61%)
  matrix products  21.2 us (14%)
  blocking collectives  17.9 us (12%)
  between operations  13.4 us (9%)
  other arithmetic  4.53 us (3%)
  local copies, waits for them, and re-layouts  3.56 us (2%)
    all_gather x1, waiting for transfers between devices, shards(): piece = lax.all_gather(normed, 'dp', axis=0, tiled=True)  53.4 us
    all_gather x1, waiting for transfers between devices, shards(): lax.all_gather(hidden, 'dp', axis=1, tiled=True)  39.8 us
    all_to_all x1, blocking collectives, shards(): lax.all_to_all(columns, 'dp', split_axis=0, concat_axis=1, tiled=True)  17.9 us
    dot_general x1, matrix products, shards(): gate = jnp.dot(piece, gate_weight, preferred_element_type=jnp.float32)  9.51 us
    dot_general x1, matrix products, shards(): jnp.dot(lax.all_gather(hidden, 'dp', axis=1, tiled=True), down_weight, pr...  8.74 us
    unnamed x6, local copies, waits for them, and re-layouts  3.56 us
  transfers between devices with their start and end apart: 2, of which 2 were waited for; matrix products, arithmetic and copies ran while one was open for 0% of the time, Pallas kernels for 0%

commit v1 on v0

v1 whole, which is shorter than its diff:
```python
import functools

import jax
import jax.numpy as jnp
from jax import lax
from jax.experimental import pallas as pl
from jax.experimental.pallas import tpu as pltpu
from jax.sharding import PartitionSpec as P

MESH = pl.DeviceIdType.MESH
CHUNKS = 8
EARLY = 4
DOWN_LOADS = 4
F32 = jnp.float32
BF16 = jnp.bfloat16


def chip_at(place, chips):
    if chips > 8:
        return place
    half = chips // 2
    back = place // half
    return (1 - back) * 2 * place + back * (2 * (chips - 1 - place) + 1)


def place_of(chip, chips):
    if chips > 8:
        return chip
    odd, rank = chip % 2, chip // 2
    return rank + odd * (chips - 1 - 2 * rank)


def block_kernel(
    n,
    tokens, gain, gate, up, down, out,
    raw, scales, gate_v, up_v, down_v, gate_acc, up_acc, hid, acc, stage,
    own_sem, gate_sem, up_sem, down_sem, scale_send, scale_recv,
    ring_recv, ring_send, sib_recv, sib_send,
    hid_recv, hid_send, hidsib_recv, hidsib_send,
    out_send, out_recv, out_own,
):
    chips = n // 2
    hops = chips // 2
    rows, width = tokens.shape
    ffl = gate.shape[1]
    cols = down.shape[1]
    depth = width // CHUNKS
    part = depth // hops
    total_rows = n * rows
    parts = hid.shape[2]
    ffe = ffl // parts
    down_rows = down.shape[0] // DOWN_LOADS

    me = lax.axis_index("dp")
    core = me % 2
    p = place_of(me // 2, chips)
    sib = me + 1 - 2 * core
    right = 2 * chip_at((p + 1) % chips, chips) + core
    left = 2 * chip_at((p + chips - 1) % chips, chips) + core
    reach = (hops - core, hops - 1 + core)

    own = pltpu.make_async_copy(tokens, raw.at[core, p], own_sem)
    own.start()

    def weight_copies(q):
        here = pl.ds(q * depth, depth)
        return (
            pltpu.make_async_copy(gate.at[here], gate_v.at[here], gate_sem.at[q]),
            pltpu.make_async_copy(up.at[here], up_v.at[here], up_sem.at[q]),
        )

    def down_copy(i):
        here = pl.ds(i * down_rows, down_rows)
        return pltpu.make_async_copy(down.at[here], down_v.at[here], down_sem.at[i])

    barrier = pltpu.get_barrier_semaphore()

    @pl.loop(1, n)
    def _(i):
        pl.semaphore_signal(barrier, inc=1, device_id={"dp": (me + i) % n}, device_id_type=MESH)

    for q in range(EARLY):
        for copy in weight_copies(q):
            copy.start()

    own.wait()
    squares = jnp.zeros((rows, 128), F32)
    step = 2048

    def add_squares(i, squares):
        wide = raw[core, p, :, pl.ds(i * step, step)].astype(F32)
        wide = wide * wide
        for b in range(step // 128):
            squares = squares + wide[:, b * 128 : (b + 1) * 128]
        return squares

    squares = lax.fori_loop(0, width // step, add_squares, squares)
    mean = jnp.sum(squares, axis=1, keepdims=True) / width
    scales[me] = jnp.broadcast_to(lax.rsqrt(mean + 1e-05), (rows, 128))
    pl.semaphore_wait(barrier, n - 1)

    def ring(k, origin, q):
        return raw.at[k, origin, :, pl.ds(q * depth, depth)]

    def send_ring(r, q, s, origin):
        pltpu.make_async_remote_copy(
            ring(core, origin, q), ring(core, origin, q), ring_send.at[q], ring_recv.at[r, q, s],
            device_id={"dp": (right, left)[r]}, device_id_type=MESH,
        ).start()

    def send_sib(q, origin):
        pltpu.make_async_remote_copy(
            ring(core, origin, q), ring(core, origin, q), sib_send.at[q], sib_recv.at[q],
            device_id={"dp": sib}, device_id_type=MESH,
        ).start()

    def wait_ring(r, q, s, origin):
        there = ring(core, origin, q)
        pltpu.make_async_copy(there, there, ring_recv.at[r, q, s - 1]).wait()

    def origin_of(r, s):
        return (p + chips - s) % chips if r == 0 else (p + s) % chips

    def first_hop(q):
        send_ring(0, q, 0, p)
        send_ring(1, q, 0, p)
        send_sib(q, p)

    slots = 2 * hops
    sends = CHUNKS * hops

    def comm(t):
        s = (t % slots) // 2
        q = 2 * (t // slots) + t % 2

        @pl.when(s == 0)
        def _():
            @pl.when(t < sends)
            def _():
                first_hop(q)

            @pl.when(t >= slots)
            def _():
                far = origin_of(0, hops)
                there = ring(core, far, q - 2)
                pltpu.make_async_copy(there, there, ring_recv.at[core, q - 2, hops - 1]).wait()
                send_sib(q - 2, far)

        @pl.when((s > 0) & (t < sends))
        def _():
            for r in range(2):
                origin = origin_of(r, s)
                wait_ring(r, q, s, origin)

                @pl.when(s < reach[r])
                def _():
                    send_ring(r, q, s, origin)

                send_sib(q, origin)

    first_hop(0)
    first_hop(1)

    @pl.loop(1, n)
    def _(i):
        pltpu.make_async_remote_copy(
            scales.at[me], scales.at[me], scale_send, scale_recv,
            device_id={"dp": (me + i) % n}, device_id_type=MESH,
        ).start()

    gate_acc[...] = jnp.zeros_like(gate_acc)
    up_acc[...] = jnp.zeros_like(up_acc)

    def compute(g):
        q = g // hops

        @pl.when(g == 0)
        def _():
            most = scales.at[pl.ds(0, n - 1)]
            pltpu.make_async_copy(most, most, scale_recv).wait()

        @pl.when(g % hops == 0)
        def _():
            for copy in weight_copies(q):
                copy.wait()
            there = raw.at[1 - core, :, :, pl.ds(q * depth, depth)]
            pltpu.make_async_copy(there, there, sib_recv.at[q]).wait()

        here = pl.ds(pl.multiple_of(g * part, 128), part)
        gains = gain[:, here]
        pieces = []
        for d in range(n):
            wide = raw[d % 2, place_of(d // 2, chips), :, here].astype(F32)
            scale = jnp.concatenate([scales[d]] * (part // 128), axis=1)
            pieces.append(wide * scale * gains)
        normed = jnp.concatenate(pieces, axis=0).astype(BF16)
        gate_acc[...] += jnp.dot(normed, gate_v[here, :], preferred_element_type=F32)
        up_acc[...] += jnp.dot(normed, up_v[here, :], preferred_element_type=F32)

    lag = slots + 1

    @pl.loop(2, sends + lag)
    def _(t):
        @pl.when(t == slots)
        def _():
            for q in range(EARLY, CHUNKS):
                for copy in weight_copies(q):
                    copy.start()

        @pl.when(t == 2 * slots)
        def _():
            for i in range(DOWN_LOADS // 2):
                down_copy(i).start()

        @pl.when(t == 3 * slots)
        def _():
            for i in range(DOWN_LOADS // 2, DOWN_LOADS):
                down_copy(i).start()

        @pl.when(t < sends + 2)
        def _():
            comm(t)

        @pl.when(t >= lag)
        def _():
            compute(t - lag)

    gates = gate_acc[...]
    hidden = (gates / (1.0 + jnp.exp(-gates)) * up_acc[...]).astype(BF16)
    for e in range(parts):
        hid[core, p, e] = hidden[:, e * ffe : (e + 1) * ffe]

    def send_hid(r, e, s, origin):
        there = hid.at[core, origin, e]
        pltpu.make_async_remote_copy(
            there, there, hid_send, hid_recv.at[r, e, s],
            device_id={"dp": (right, left)[r]}, device_id_type=MESH,
        ).start()

    def send_hidsib(e, s, origin):
        there = hid.at[core, origin, e]
        pltpu.make_async_remote_copy(
            there, there, hidsib_send, hidsib_recv.at[e, s],
            device_id={"dp": sib}, device_id_type=MESH,
        ).start()

    for e in range(parts):
        send_hid(0, e, 0, p)
        send_hid(1, e, 0, p)
        send_hidsib(e, 0, p)
    for i in range(DOWN_LOADS):
        down_copy(i).wait()
    acc[...] = jnp.zeros_like(acc)

    def add_block(origin, e):
        first = 2 * chip_at(origin, chips)
        for k in range(2):
            here = pl.ds(pl.multiple_of((first + k) * ffl + e * ffe, 128), ffe)
            acc[...] += jnp.dot(hid[k, origin, e], down_v[here, :], preferred_element_type=F32)

    def wait_hidsib(e, u, blocks):
        there = hid.at[0, pl.ds(0, blocks), e]
        pltpu.make_async_copy(there, there, hidsib_recv.at[e, u]).wait()

    @pl.loop(1, hops + 2)
    def _(s):
        u = s - 1
        for e in range(parts):
            @pl.when(s < hops)
            def _():
                for r in range(2):
                    origin = origin_of(r, s)
                    there = hid.at[core, origin, e]
                    pltpu.make_async_copy(there, there, hid_recv.at[r, e, s - 1]).wait()

                    @pl.when(s < reach[r])
                    def _():
                        send_hid(r, e, s, origin)

                    send_hidsib(e, s, origin)

            @pl.when(s == hops)
            def _():
                far = origin_of(0, hops)
                there = hid.at[core, far, e]
                pltpu.make_async_copy(there, there, hid_recv.at[core, e, hops - 1]).wait()
                send_hidsib(e, hops, far)

            @pl.when((u == 0) | (u == hops))
            def _():
                wait_hidsib(e, u, 1)

            @pl.when((u > 0) & (u < hops))
            def _():
                wait_hidsib(e, u, 2)
                add_block(origin_of(1, u), e)

            add_block(origin_of(0, u), e)

    mine = pl.ds(pl.multiple_of(me * cols, 128), cols)
    for d in range(n):
        wide = raw[d % 2, place_of(d // 2, chips), :, mine].astype(F32)
        stage[d] = (wide + acc[d * rows : (d + 1) * rows, :]).astype(BF16)

    @pl.loop(1, n)
    def _(i):
        peer = (me + i) % n
        pltpu.make_async_remote_copy(
            stage.at[peer], out.at[:, mine], out_send, out_recv,
            device_id={"dp": peer}, device_id_type=MESH,
        ).start()

    keep = pltpu.make_async_copy(stage.at[me], out.at[:, mine], out_own)
    keep.start()

    most = scales.at[pl.ds(0, n - 1)]
    pltpu.make_async_copy(most, most, scale_send).wait()
    for q in range(CHUNKS):
        there = raw.at[0, pl.ds(0, chips - 1), :, pl.ds(q * depth, depth)]
        pltpu.make_async_copy(there, there, ring_send.at[q]).wait()
        there = raw.at[0, :, :, pl.ds(q * depth, depth)]
        pltpu.make_async_copy(there, there, sib_send.at[q]).wait()
    there = hid.at[0, pl.ds(0, chips - 1)]
    pltpu.make_async_copy(there, there, hid_send).wait()
    there = hid.at[0]
    pltpu.make_async_copy(there, there, hidsib_send).wait()
    keep.wait()
    there = stage.at[pl.ds(0, n - 1)]
    pltpu.make_async_copy(there, there, out_send).wait()
    pltpu.make_async_copy(there, there, out_recv).wait()


def shards(n, tokens, gain, gate_weight, up_weight, down_weight):
    rows, width = tokens.shape
    ffl = gate_weight.shape[1]
    ff, cols = down_weight.shape
    chips = n // 2
    hops = chips // 2
    parts = 2 if ffl >= 256 else 1
    total_rows = n * rows
    dma = pltpu.SemaphoreType.DMA
    hbm = pl.BlockSpec(memory_space=pl.ANY)
    wide_gain = gain.astype(F32).reshape(1, width)
    return pl.pallas_call(
        functools.partial(block_kernel, n),
        out_shape=jax.ShapeDtypeStruct((rows, width), BF16),
        in_specs=[hbm, pl.BlockSpec(memory_space=pltpu.VMEM), hbm, hbm, hbm],
        out_specs=hbm,
        scratch_shapes=[
            pltpu.VMEM((2, chips, rows, width), BF16),
            pltpu.VMEM((n, rows, 128), F32),
            pltpu.VMEM((width, ffl), BF16),
            pltpu.VMEM((width, ffl), BF16),
            pltpu.VMEM((ff, cols), BF16),
            pltpu.VMEM((total_rows, ffl), F32),
            pltpu.VMEM((total_rows, ffl), F32),
            pltpu.VMEM((2, chips, parts, total_rows, ffl // parts), BF16),
            pltpu.VMEM((total_rows, cols), F32),
            pltpu.VMEM((n, rows, cols), BF16),
            dma(()),
            dma((CHUNKS,)),
            dma((CHUNKS,)),
            dma((DOWN_LOADS,)),
            dma(()),
            dma(()),
            dma((2, CHUNKS, hops)),
            dma((CHUNKS,)),
            dma((CHUNKS,)),
            dma((CHUNKS,)),
            dma((2, parts, hops)),
            dma(()),
            dma((parts, hops + 1)),
            dma(()),
            dma(()),
            dma(()),
            dma(()),
        ],
        compiler_params=pltpu.CompilerParams(
            collective_id=0, has_side_effects=True, vmem_limit_bytes=62 * 1024 * 1024
        ),
        cost_estimate=pl.CostEstimate(
            flops=2 * total_rows * (2 * width * ffl + ff * cols),
            bytes_accessed=2 * (2 * width * ffl + ff * cols),
            transcendentals=total_rows * ffl,
        ),
        name="swiglu_block",
    )(tokens, wide_gain, gate_weight, up_weight, down_weight)


def solution(mesh):
    return jax.shard_map(
        functools.partial(shards, mesh.shape["dp"]),
        mesh=mesh,
        in_specs=(P(("groups", "dp"), None), P(), P(None, "dp"), P(None, "dp"), P(None, "dp")),
        out_specs=P(("groups", "dp"), None),
        check_vma=False,
    )
```

time: 154 us -> 83.1 us (0.54)
  waiting for transfers between devices: 93.2 us -> 0 us
  Pallas kernels: 0 us -> 79.7 us
  matrix products: 21.2 us -> 0 us
  blocking collectives: 17.9 us -> 0 us
  between operations: 13.4 us -> 0.01 us
  other arithmetic: 4.53 us -> 1.39 us
  local copies, waits for them, and re-layouts: 3.56 us -> 1.67 us
    all_gather x2 -> x0, waiting for transfers between devices: 93.2 us -> none  [the longest x1 53.4 us: shards(): piece = lax.all_gather(normed, 'dp', axis=0, tiled=True)]
    pallas_call x0 -> x1, Pallas kernels: none -> 79.7 us  [shards(): pl.pallas_call(functools.partial(block_kernel, n), out_shape=jax.ShapeDty...]
    dot_general x3 -> x0, matrix products: 21.2 us -> none  [the longest x1 9.51 us: shards(): gate = jnp.dot(piece, gate_weight, preferred_element_type=jnp.float32)]
    all_to_all x1 -> x0, blocking collectives: 17.9 us -> none  [shards(): lax.all_to_all(columns, 'dp', split_axis=0, concat_axis=1, tiled=True)]
    convert_element_type x3 -> x0, other arithmetic: 3.32 us -> none  [the longest x2 2.55 us: shards(): normed = (wide * scale * gain.astype(jnp.float32)).astype(jnp.bfloat16)]
    unnamed x6 -> x1, local copies, waits for them, and re-layouts: 3.56 us -> 1.67 us
  transfers between devices with their start and end apart: 2 -> 0, of which waited for: 2 -> 0; matrix products, arithmetic and copies ran while one was open for 0% -> 0% of each run, Pallas kernels for 0% -> 0%
where the time goes in v1:
time: 83.1 us; the launch traced here: 82.8 us
  Pallas kernels  79.7 us (96%)
  local copies, waits for them, and re-layouts  1.67 us (2%)
  other arithmetic  1.39 us (2%)
    pallas_call x1, Pallas kernels, shards(): pl.pallas_call(functools.partial(block_kernel, n), out_shape=jax.ShapeDty...  79.7 us
    unnamed x1, local copies, waits for them, and re-layouts  1.67 us

profile of v1, /device:TPU:0, one launch (start us, length us, event | category | flops | bytes accessed | tf_op | source)
XLA Modules:
  0.0 82.8 jit_solution(11900285810786854930)
XLA Ops:
  0.0 1.4 %reshape.7 = f32[16384]{0:T(1024)} convert(bf16[16384]{0:T(1024)(128)(2,1)} %param.6) | non-fusion elementwise | flops 16384 | bytes 98304 | tf_op jit(solution)/shard_map/reshape | solution.py:343
  1.4 79.7 %swiglu_block.1 = bf16[8,16384]{1,0:T(8,128)(2,1)} custom-call(bf16[8,16384]{1,0:T(8,128)(2,1)} %tokens.1, f32[1,16384]{1,0:T(1,128)} %bitcast.1, bf16[16384,512]{1,0:T(8,128)(2,1)} %gate.1, bf16[16384,512]{1,0:T(8,128)(2,1)} %up.1, bf16[8192,1024]{1,0:T(8,128)(2,1)} %down.1), custom_call_target="tpu_custom_call" | custom-call | flops 6442450944 | bytes 50331648 | tf_op jit(solution)/shard_map/swiglu_block/pallas_call | solution.py:344
  81.1 1.7 %copy.7 = bf16[8,16384]{1,0:T(8,128)(2,1)} copy(bf16[8,16384]{1,0:T(8,128)(2,1)} %swiglu_block.1) | data formatting | bytes 524288

commit v2 on v1

--- a/solution.py
+++ b/solution.py
@@ -8,9 +8,11 @@
 from jax.sharding import PartitionSpec as P
 
 MESH = pl.DeviceIdType.MESH
-CHUNKS = 8
-EARLY = 4
+CHUNKS = 4
+EARLY = 2
 DOWN_LOADS = 4
+LEAD = 2
+STAGGER = 1
 F32 = jnp.float32
 BF16 = jnp.bfloat16
 
@@ -126,27 +128,8 @@
         send_ring(1, q, 0, p)
         send_sib(q, p)
 
-    slots = 2 * hops
-    sends = CHUNKS * hops
-
-    def comm(t):
-        s = (t % slots) // 2
-        q = 2 * (t // slots) + t % 2
-
-        @pl.when(s == 0)
-        def _():
-            @pl.when(t < sends)
-            def _():
-                first_hop(q)
-
-            @pl.when(t >= slots)
-            def _():
-                far = origin_of(0, hops)
-                there = ring(core, far, q - 2)
-                pltpu.make_async_copy(there, there, ring_recv.at[core, q - 2, hops - 1]).wait()
-                send_sib(q - 2, far)
-
-        @pl.when((s > 0) & (t < sends))
+    def comm(q, s):
+        @pl.when(s < hops)
         def _():
             for r in range(2):
                 origin = origin_of(r, s)
@@ -158,8 +141,14 @@
 
                 send_sib(q, origin)
 
-    first_hop(0)
-    first_hop(1)
+        @pl.when(s == hops)
+        def _():
+            far = origin_of(0, hops)
+            wait_ring(core, q, hops, far)
+            send_sib(q, far)
+
+    for q in range(LEAD + 1):
+        first_hop(q)
 
     @pl.loop(1, n)
     def _(i):
@@ -197,33 +186,32 @@
         gate_acc[...] += jnp.dot(normed, gate_v[here, :], preferred_element_type=F32)
         up_acc[...] += jnp.dot(normed, up_v[here, :], preferred_element_type=F32)
 
-    lag = slots + 1
-
-    @pl.loop(2, sends + lag)
+    @pl.loop(1, CHUNKS + STAGGER * hops + 1)
     def _(t):
-        @pl.when(t == slots)
-        def _():
-            for q in range(EARLY, CHUNKS):
-                for copy in weight_copies(q):
-                    copy.start()
-
-        @pl.when(t == 2 * slots)
-        def _():
-            for i in range(DOWN_LOADS // 2):
-                down_copy(i).start()
-
-        @pl.when(t == 3 * slots)
-        def _():
-            for i in range(DOWN_LOADS // 2, DOWN_LOADS):
-                down_copy(i).start()
-
-        @pl.when(t < sends + 2)
-        def _():
-            comm(t)
-
-        @pl.when(t >= lag)
-        def _():
-            compute(t - lag)
+        @pl.when(t + LEAD < CHUNKS)
+        def _():
+            first_hop(t + LEAD)
+
+        @pl.when(t <= CHUNKS - EARLY)
+        def _():
+            for copy in weight_copies(t + EARLY - 1):
+                copy.start()
+
+        @pl.when((t > CHUNKS - EARLY) & (t <= CHUNKS - EARLY + DOWN_LOADS))
+        def _():
+            down_copy(t - (CHUNKS - EARLY) - 1).start()
+
+        @pl.loop(1, hops + 1)
+        def _(s):
+            q = t - STAGGER * s
+
+            @pl.when((q >= 0) & (q < CHUNKS))
+            def _():
+                comm(q, s)
+
+            @pl.when(t > STAGGER * hops)
+            def _():
+                compute((t - STAGGER * hops - 1) * hops + s - 1)
 
     gates = gate_acc[...]
     hidden = (gates / (1.0 + jnp.exp(-gates)) * up_acc[...]).astype(BF16)
@@ -252,11 +240,16 @@
         down_copy(i).wait()
     acc[...] = jnp.zeros_like(acc)
 
+    group = 2 if parts > 1 else 1
+
     def add_block(origin, e):
         first = 2 * chip_at(origin, chips)
+        total = acc[...]
         for k in range(2):
-            here = pl.ds(pl.multiple_of((first + k) * ffl + e * ffe, 128), ffe)
-            acc[...] += jnp.dot(hid[k, origin, e], down_v[here, :], preferred_element_type=F32)
+            here = pl.ds(pl.multiple_of((first + k) * ffl + e * ffe, 128), group * ffe)
+            block = jnp.concatenate([hid[k, origin, e + i] for i in range(group)], axis=1)
+            total += jnp.dot(block, down_v[here, :], preferred_element_type=F32)
+        acc[...] = total
 
     def wait_hidsib(e, u, blocks):
         there = hid.at[0, pl.ds(0, blocks), e]
@@ -265,7 +258,8 @@
     @pl.loop(1, hops + 2)
     def _(s):
         u = s - 1
-        for e in range(parts):
+
+        def hop(e):
             @pl.when(s < hops)
             def _():
                 for r in range(2):
@@ -293,6 +287,13 @@
             @pl.when((u > 0) & (u < hops))
             def _():
                 wait_hidsib(e, u, 2)
+
+        for e in range(0, parts, group):
+            for i in range(group):
+                hop(e + i)
+
+            @pl.when((u > 0) & (u < hops))
+            def _():
                 add_block(origin_of(1, u), e)
 
             add_block(origin_of(0, u), e)
@@ -336,7 +337,7 @@
     ff, cols = down_weight.shape
     chips = n // 2
     hops = chips // 2
-    parts = 2 if ffl >= 256 else 1
+    parts = 4 if ffl % 512 == 0 else 1
     total_rows = n * rows
     dma = pltpu.SemaphoreType.DMA
     hbm = pl.BlockSpec(memory_space=pl.ANY)

time: 83.1 us -> 61.9 us (0.74)
  Pallas kernels: 79.7 us -> 58.6 us
    pallas_call x1, Pallas kernels: 79.7 us -> 58.6 us  [shards(): pl.pallas_call(functools.partial(block_kernel, n), out_shape=jax.ShapeDty...]
where the time goes in v2:
time: 61.9 us; the launch traced here: 61.7 us
  Pallas kernels  58.6 us (95%)
  local copies, waits for them, and re-layouts  1.67 us (3%)
  other arithmetic  1.39 us (2%)
    pallas_call x1, Pallas kernels, shards(): pl.pallas_call(functools.partial(block_kernel, n), out_shape=jax.ShapeDty...  58.6 us
    unnamed x1, local copies, waits for them, and re-layouts  1.67 us
    reshape x1, other arithmetic, shards(): wide_gain = gain.astype(F32).reshape(1, width)  1.39 us

profile of v2, /device:TPU:0, one launch (start us, length us, event | category | flops | bytes accessed | tf_op | source)
XLA Modules:
  0.0 61.7 jit_solution(13794848687101455058)
XLA Ops:
  0.0 1.4 %reshape.7 = f32[16384]{0:T(1024)} convert(bf16[16384]{0:T(1024)(128)(2,1)} %param.6) | non-fusion elementwise | flops 16384 | bytes 98304 | tf_op jit(solution)/shard_map/reshape | solution.py:344
  1.4 58.6 %swiglu_block.1 = bf16[8,16384]{1,0:T(8,128)(2,1)} custom-call(bf16[8,16384]{1,0:T(8,128)(2,1)} %tokens.1, f32[1,16384]{1,0:T(1,128)} %bitcast.1, bf16[16384,512]{1,0:T(8,128)(2,1)} %gate.1, bf16[16384,512]{1,0:T(8,128)(2,1)} %up.1, bf16[8192,1024]{1,0:T(8,128)(2,1)} %down.1), custom_call_target="tpu_custom_call" | custom-call | flops 6442450944 | bytes 50331648 | tf_op jit(solution)/shard_map/swiglu_block/pallas_call | solution.py:345
  60.0 1.7 %copy.7 = bf16[8,16384]{1,0:T(8,128)(2,1)} copy(bf16[8,16384]{1,0:T(8,128)(2,1)} %swiglu_block.1) | data formatting | bytes 524288

commit v3 on v2

--- a/solution.py
+++ b/solution.py
@@ -34,7 +34,7 @@
 
 def block_kernel(
     n,
-    tokens, gain, gate, up, down, out,
+    tokens, gain_in, gate, up, down, out, gain,
     raw, scales, gate_v, up_v, down_v, gate_acc, up_acc, hid, acc, stage,
     own_sem, gate_sem, up_sem, down_sem, scale_send, scale_recv,
     ring_recv, ring_send, sib_recv, sib_send,
@@ -85,6 +85,7 @@
         for copy in weight_copies(q):
             copy.start()
 
+    gain[...] = gain_in[...].astype(F32).reshape(1, width)
     own.wait()
     squares = jnp.zeros((rows, 128), F32)
     step = 2048
@@ -341,13 +342,13 @@
     total_rows = n * rows
     dma = pltpu.SemaphoreType.DMA
     hbm = pl.BlockSpec(memory_space=pl.ANY)
-    wide_gain = gain.astype(F32).reshape(1, width)
     return pl.pallas_call(
         functools.partial(block_kernel, n),
         out_shape=jax.ShapeDtypeStruct((rows, width), BF16),
         in_specs=[hbm, pl.BlockSpec(memory_space=pltpu.VMEM), hbm, hbm, hbm],
         out_specs=hbm,
         scratch_shapes=[
+            pltpu.VMEM((1, width), F32),
             pltpu.VMEM((2, chips, rows, width), BF16),
             pltpu.VMEM((n, rows, 128), F32),
             pltpu.VMEM((width, ffl), BF16),
@@ -385,7 +386,7 @@
             transcendentals=total_rows * ffl,
         ),
         name="swiglu_block",
-    )(tokens, wide_gain, gate_weight, up_weight, down_weight)
+    )(tokens, gain, gate_weight, up_weight, down_weight)
 
 
 def solution(mesh):

time: 61.9 us -> 60.4 us (0.976)
  other arithmetic: 1.39 us -> 0 us
    reshape x1 -> x0, other arithmetic: 1.39 us -> none  [shards(): wide_gain = gain.astype(F32).reshape(1, width)]
where the time goes in v3:
time: 60.4 us; the launch traced here: 60.2 us
  Pallas kernels  58.5 us (97%)
  local copies, waits for them, and re-layouts  1.67 us (3%)
    pallas_call x1, Pallas kernels, shards(): pl.pallas_call(functools.partial(block_kernel, n), out_shape=jax.ShapeDty...  58.5 us
    unnamed x1, local copies, waits for them, and re-layouts  1.67 us

profile of v3, /device:TPU:0, one launch (start us, length us, event | category | flops | bytes accessed | tf_op | source)
XLA Modules:
  0.0 60.2 jit_solution(5009873558913368368)
XLA Ops:
  0.0 58.5 %swiglu_block.1 = bf16[8,16384]{1,0:T(8,128)(2,1)} custom-call(bf16[8,16384]{1,0:T(8,128)(2,1)} %tokens.1, bf16[16384]{0:T(1024)(128)(2,1)} %gain_in.1, bf16[16384,512]{1,0:T(8,128)(2,1)} %gate.1, bf16[16384,512]{1,0:T(8,128)(2,1)} %up.1, bf16[8192,1024]{1,0:T(8,128)(2,1)} %down.1), custom_call_target="tpu_custom_call" | custom-call | flops 6442450944 | bytes 50331648 | tf_op jit(solution)/shard_map/swiglu_block/pallas_call | solution.py:345
  58.5 1.7 %copy.7 = bf16[8,16384]{1,0:T(8,128)(2,1)} copy(bf16[8,16384]{1,0:T(8,128)(2,1)} %swiglu_block.1) | data formatting | bytes 524288
